TPU v7x, 256 devices: a whole 4x4x8 slice. The times are simulated.
256 devices in a mesh: row: 32 (over x, y, core), col: 8 (over z).
Axes of the slice: x: 4, y: 4, z: 8, core: 2. Of those that a mesh axis runs over, the one named last changes fastest.
Arguments:
- tokens: bfloat16 [512, 8192], P('row', 'col'), may hold values from -6 to 6
- gate_up: bfloat16 [8192, 2, 28672], P('col', None, 'row'), may hold values from -0.0625 to 0.0625
- down: bfloat16 [28672, 8192], P('row', 'col'), may hold values from -0.03125 to 0.03125
- target: bfloat16 [512, 8192], P('row', 'col'), may hold values from -6 to 6
Outputs:
- output: bfloat16 [512, 8192], P('row', 'col')
- grad_tokens: bfloat16 [512, 8192], P('row', 'col')
- grad_gate_up: bfloat16 [8192, 2, 28672], P('col', None, 'row')
- grad_down: bfloat16 [28672, 8192], P('row', 'col')
All inputs are finite; a program needn't handle non-finite values.
Results may differ from a plain program's by a relative error of at most 0.04.
Values may be sent and summed in bfloat16 or wider, within the bound.
No kernel may reach another device: no remote copies, remote signals or barrier semaphores. Data moves between devices by JAX's collectives and lax.ppermute only.
A program may use at most 64 MiB of HBM per device.

v0:
```python
import jax
import jax.numpy as jnp
from jax import lax
from jax.sharding import PartitionSpec as P


def gather_rows(value):
    return lax.all_gather(value, "row", axis=0, tiled=True)


def gather_cols(value):
    return lax.all_gather(value, "col", axis=0, tiled=True)


def scatter_cols(value):
    return lax.psum_scatter(
        value.astype(jnp.bfloat16), "col", scatter_dimension=0, tiled=True
    ).astype(jnp.float32)


def scatter_rows(value):
    return lax.psum_scatter(
        value.astype(jnp.bfloat16), "row", scatter_dimension=0, tiled=True
    ).astype(jnp.float32)


def row_sum(term_fn, total_rows):
    return scatter_rows(term_fn(0, total_rows))


def swiglu_grad(grad_hidden, gate, up):
    sigma = jax.nn.sigmoid(gate)
    grad_gate = grad_hidden * up * sigma * (1.0 + gate * (1.0 - sigma))
    grad_up = grad_hidden * gate * sigma
    return jnp.stack([grad_gate, grad_up], axis=1).astype(jnp.bfloat16)


def per_device(tokens, gate_up, down, target):
    all_tokens = gather_rows(tokens)
    total_rows = all_tokens.shape[0]
    partial_value = jnp.einsum(
        "td,dgf->tgf", all_tokens, gate_up, preferred_element_type=jnp.float32
    )
    projected = scatter_cols(partial_value)
    gate = projected[:, 0]
    up = projected[:, 1]
    hidden = (jax.nn.silu(gate) * up).astype(jnp.bfloat16)
    all_hidden = gather_cols(hidden)

    def mixed_term(start, count):
        return jnp.dot(all_hidden, down, preferred_element_type=jnp.float32)

    mixed = row_sum(mixed_term, total_rows)
    output = (tokens.astype(jnp.float32) + mixed).astype(jnp.bfloat16)
    delta = (output.astype(jnp.float32) - target.astype(jnp.float32)).astype(jnp.bfloat16)
    all_delta = gather_rows(delta)
    hidden_part = jnp.einsum("td,fd->tf", all_delta, down, preferred_element_type=jnp.float32)
    grad_down = jnp.einsum(
        "tf,td->fd", all_hidden, all_delta, preferred_element_type=jnp.float32
    ).astype(jnp.bfloat16)
    grad_hidden = scatter_cols(hidden_part)
    all_grad = gather_cols(swiglu_grad(grad_hidden, gate, up))
    grad_gate_up = jnp.einsum(
        "td,tgf->dgf", all_tokens, all_grad, preferred_element_type=jnp.float32
    ).astype(jnp.bfloat16)

    def inner_term(start, count):
        return jnp.einsum("tgf,dgf->td", all_grad, gate_up, preferred_element_type=jnp.float32)

    grad_inner = row_sum(inner_term, total_rows)
    grad_tokens = (delta.astype(jnp.float32) + grad_inner).astype(jnp.bfloat16)
    return (output, grad_tokens, grad_gate_up, grad_down)


def solution(mesh):
    in_specs = (P("row", "col"), P("col", None, "row"), P("row", "col"), P("row", "col"))
    out_specs = (P("row", "col"), P("row", "col"), P("col", None, "row"), P("row", "col"))
    return jax.shard_map(
        per_device, mesh=mesh, in_specs=in_specs, out_specs=out_specs, check_vma=False
    )
```

profile of v0, /device:TPU:2, one launch (start us, length us, event | category | flops | bytes accessed | tf_op | source)
XLA Modules:
  0.0 452.4 jit_solution(11210774648093839620)
XLA Ops:
  7.2 0.7 all-gather.4.cloned.1.call-update
  8.0 53.1 %all-gather.4.cloned.1.call-done = bf16[512,1024]{1,0:T(8,128)(2,1)} async-done(((bf16[16,1024]{1,0:T(8,128)(2,1)}), bf16[512,1024]{1,0:T(8,128)(2,1)}) %all-gather.4.cloned.1.call-update) | async-done | bytes 1048592 | tf_op jit(solution)/shard_map/all_gather | solution.py:8
  61.0 5.7 %fusion.4 = bf16[512,2,896]{2,0,1:T(8,128)(2,1)} fusion(bf16[1024,2,896]{2,1,0:T(2,128)(2,1)} %param.5, bf16[512,1024]{1,0:T(8,128)(2,1)} %all-gather.4.cloned.1.call-done), kind=kOutput, calls=%fused_computation.6 | convolution fusion | flops 1879965696 | bytes 6553600 | tf_op jit(solution)/shard_map/td,dgf->tgf/dot_general | solution.py:41
  66.8 41.1 %reduce-scatter.5.cloned.1.call-done = bf16[64,2,896]{2,0,1:T(8,128)(2,1)} async-done(((bf16[512,2,896]{2,0,1:T(8,128)(2,1)}), bf16[64,2,896]{2,0,1:T(8,128)(2,1)}) %reduce-scatter.5.cloned.1.call-update) | async-done | bytes 229392 | tf_op jit(solution)/shard_map/reduce_scatter | solution.py:16
  107.8 1.0 convert_element_type.60
  108.8 0.1 multiply_convert_fusion
  108.9 26.3 %all_gather.13 = bf16[512,896]{1,0:T(8,128)(2,1)S(1)} all-gather(bf16[64,896]{1,0:T(8,128)(2,1)S(1)} %multiply_convert_fusion), channel_id=1, replica_groups=mesh['row'=32,'col'=8] {'col'}, dimensions={0}, use_global_device_ids=true | all-gather | bytes 1032192 | tf_op jit(solution)/shard_map/all_gather | solution.py:12
  135.2 2.2 convolution_convert_fusion.1
  137.5 0.0 all-gather.6.cloned.1.call-start
  137.5 84.0 %reduce-scatter.7.cloned.1.call-done = bf16[16,1024]{1,0:T(8,128)(2,1)} async-done(((bf16[512,1024]{1,0:T(8,128)(2,1)}), bf16[16,1024]{1,0:T(8,128)(2,1)}) %reduce-scatter.7.cloned.1.call-update) | async-done | bytes 32784 | tf_op jit(solution)/shard_map/reduce_scatter | solution.py:22
  221.5 1.4 subtract_convert_fusion
  222.9 0.0 reduce-scatter.9.cloned.1.call-start
  223.0 49.1 %all-gather.6.cloned.1.call-done = bf16[512,1024]{1,0:T(8,128)(2,1)} async-done(((bf16[16,1024]{1,0:T(8,128)(2,1)}), bf16[512,1024]{1,0:T(8,128)(2,1)}) %all-gather.6.cloned.1.call-update) | async-done | bytes 1048592 | tf_op jit(solution)/shard_map/all_gather | solution.py:8
  272.0 3.4 convolution_convert_fusion.2
  275.5 38.0 %reduce-scatter.9.cloned.1.call-done = bf16[64,896]{1,0:T(8,128)(2,1)} async-done(((bf16[512,896]{1,0:T(8,128)(2,1)}), bf16[64,896]{1,0:T(8,128)(2,1)}) %reduce-scatter.9.cloned.1.call-update) | async-done | bytes 114704 | tf_op jit(solution)/shard_map/reduce_scatter | solution.py:16
  313.5 1.0 fusion.17
  314.5 0.7 pad_maximum_fusion
  315.3 39.7 %all-gather.8.cloned.1.call-done = bf16[512,2,896]{2,0,1:T(8,128)(2,1)} async-done(((bf16[64,2,896]{2,0,1:T(8,128)(2,1)}), bf16[512,2,896]{2,0,1:T(8,128)(2,1)}) %all-gather.8.cloned.1.call-update) | async-done | bytes 1835024 | tf_op jit(solution)/shard_map/all_gather | solution.py:12
  355.0 5.7 %bitcast_convert_fusion = bf16[512,1024]{1,0:T(8,128)(2,1)} fusion(bf16[512,2,896]{2,0,1:T(8,128)(2,1)} %all-gather.8.cloned.1.call-done, bf16[1024,2,896]{2,1,0:T(2,128)(2,1)} %param.5), kind=kOutput, calls=%fused_computation.5 | convolution fusion | flops 1879572480 | bytes 6553600 | tf_op jit(solution)/shard_map/tgf,dgf->td/dot_general | solution.py:68
  360.7 3.8 convolution_convert_fusion
  364.4 3.9 convert_bitcast_fusion
  368.3 10.0 %copy.10 = bf16[1024,2,896]{2,1,0:T(2,128)(2,1)} copy(bf16[1024,2,896]{0,2,1:T(8,128)(2,1)} %convert_bitcast_fusion) | data formatting | bytes 7340032
  378.3 65.9 %reduce-scatter.11.cloned.1.call-done = bf16[16,1024]{1,0:T(8,128)(2,1)} async-done(((bf16[512,1024]{1,0:T(8,128)(2,1)}), bf16[16,1024]{1,0:T(8,128)(2,1)}) %reduce-scatter.11.cloned.1.call-update) | async-done | bytes 32784 | tf_op jit(solution)/shard_map/reduce_scatter | solution.py:22
  444.2 1.4 add_convert_fusion
  (23 shorter events, 0.3 us)
Async XLA Ops:
  7.2 128.0 %copy-start = (bf16[896,1024]{1,0:T(8,128)(2,1)S(1)}, bf16[896,1024]{1,0:T(8,128)(2,1)}, u32[]{:S(2)}) copy-start(bf16[896,1024]{1,0:T(8,128)(2,1)} %param.6) | copy-start | bytes 5505028
  7.2 53.8 %all-gather.4.cloned.1.call-start = ((), (), s32[]{:S(2)}) async-start(), calls=%async_computation.4 | async-start | bytes 1081344 | tf_op jit(solution)/shard_map/all_gather | solution.py:8
  7.9 99.9 %reduce-scatter.5.cloned.1.call-start = ((), (), s32[]{:S(2)}) async-start(), calls=%async_computation.5 | async-start | bytes 2064384 | tf_op jit(solution)/shard_map/reduce_scatter | solution.py:16
  66.7 154.8 %reduce-scatter.7.cloned.1.call-start = ((), (), s32[]{:S(2)}) async-start(), calls=%async_computation.6 | async-start | bytes 1081344 | tf_op jit(solution)/shard_map/reduce_scatter | solution.py:22
  135.2 86.3 %copy-start.2 = (bf16[16,1024]{1,0:T(8,128)(2,1)S(1)}, bf16[16,1024]{1,0:T(8,128)(2,1)}, u32[]{:S(2)}) copy-start(bf16[16,1024]{1,0:T(8,128)(2,1)} %param.4) | copy-start | bytes 98308
  135.2 86.3 %copy-start.3 = (bf16[16,1024]{1,0:T(8,128)(2,1)S(1)}, bf16[16,1024]{1,0:T(8,128)(2,1)}, u32[]{:S(2)}) copy-start(bf16[16,1024]{1,0:T(8,128)(2,1)} %param.7) | copy-start | bytes 98308
  137.5 134.6 %all-gather.6.cloned.1.call-start = ((), (), s32[]{:S(2)}) async-start(), calls=%async_computation.7 | async-start | bytes 1081344 | tf_op jit(solution)/shard_map/all_gather | solution.py:8
  222.9 90.6 %reduce-scatter.9.cloned.1.call-start = ((), (), s32[]{:S(2)}) async-start(), calls=%async_computation.8 | async-start | bytes 1032192 | tf_op jit(solution)/shard_map/reduce_scatter | solution.py:16
  275.5 79.5 %all-gather.8.cloned.1.call-start = ((), (), s32[]{:S(2)}) async-start(), calls=%async_computation.9 | async-start | bytes 2064384 | tf_op jit(solution)/shard_map/all_gather | solution.py:12
  315.2 129.0 %reduce-scatter.11.cloned.1.call-start = ((), (), s32[]{:S(2)}) async-start(), calls=%async_computation.10 | async-start | bytes 1081344 | tf_op jit(solution)/shard_map/reduce_scatter | solution.py:22
  360.7 3.8 copy-start.4
  360.7 3.8 copy-start.5
  368.3 75.9 %copy-start.1 = (bf16[16,1024]{1,0:T(8,128)(2,1)S(1)}, bf16[16,1024]{1,0:T(8,128)(2,1)}, u32[]{:S(2)}) copy-start(bf16[16,1024]{1,0:T(8,128)(2,1)} %get-tuple-element.8) | copy-start | bytes 98308
Sparse Core Ops, SparseCore 0:
  10.6 50.4 all-gather.3
  66.8 40.9 reduce-scatter.4
  137.6 83.8 reduce-scatter.6
  224.8 47.1 all-gather.5
  275.6 37.8 reduce-scatter.8
  315.7 39.1 all-gather.7
  360.8 83.3 reduce-scatter.10
where the time goes:
time: 453 us; the launch traced here: 452 us
  waiting for transfers between devices  371 us (82%)
  blocking collectives  26.3 us (6%)
  matrix products  24.6 us (5%)
  between operations  14.2 us (3%)
  local copies, waits for them, and re-layouts  10 us (2%)
  other arithmetic  5.54 us (1%)
    reduce_scatter x2, waiting for transfers between devices, scatter_rows(): lax.psum_scatter(value.astype(jnp.bfloat16), 'row', scatter_dimension=0,...  150 us
    all_gather x2, waiting for transfers between devices, gather_rows(): return lax.all_gather(value, 'row', axis=0, tiled=True)  102 us
    reduce_scatter x2, waiting for transfers between devices, scatter_cols(): lax.psum_scatter(value.astype(jnp.bfloat16), 'col', scatter_dimension=0,...  79 us
    all_gather x1, waiting for transfers between devices, gather_cols(): return lax.all_gather(value, 'col', axis=0, tiled=True)  39.7 us
    all_gather x1, blocking collectives, gather_cols(): return lax.all_gather(value, 'col', axis=0, tiled=True)  26.3 us
    unnamed x13, local copies, waits for them, and re-layouts  10 us
  transfers between devices with their start and end apart: 7, of which 7 were waited for; matrix products, arithmetic and copies ran while one was open for 4% of the time, Pallas kernels for 0%

commit v1 on v0

--- a/solution.py
+++ b/solution.py
@@ -5,7 +5,16 @@
 
 
 def gather_rows(value):
-    return lax.all_gather(value, "row", axis=0, tiled=True)
+
+    def recover_rails(local_array, join_dim):
+        runs = []
+        for _ in range(lax.axis_size("row")):
+            runs.append(local_array)
+        met_up = jnp.stack(runs)
+        inter = lax.all_to_all(met_up, axis_name="row", split_axis=0, concat_axis=0)
+        return jnp.concatenate(inter, axis=join_dim)
+
+    return recover_rails(value, 0)
 
 
 def gather_cols(value):

time: 453 us -> 396 us (0.87)
  waiting for transfers between devices: 371 us -> 271 us
  blocking collectives: 26.3 us -> 68.1 us
    all_gather x2 -> x0, waiting for transfers between devices: 102 us -> none  [gather_rows(): return lax.all_gather(value, 'row', axis=0, tiled=True)]
    all_to_all x0 -> x2, blocking collectives: none -> 41.9 us  [recover_rails(): inter = lax.all_to_all(met_up, axis_name='row', split_axis=0, concat_axis=0)]
  transfers between devices with their start and end apart: 7 -> 5, of which waited for: 7 -> 5; matrix products, arithmetic and copies ran while one was open for 4% -> 5% of each run, Pallas kernels for 0% -> 0%
where the time goes in v1:
time: 396 us; the launch traced here: 395 us
  waiting for transfers between devices  271 us (68%)
  blocking collectives  68.1 us (17%)
  matrix products  23.4 us (6%)
  between operations  13.8 us (3%)
  local copies, waits for them, and re-layouts  13 us (3%)
  other arithmetic  5.54 us (1%)
    reduce_scatter x2, waiting for transfers between devices, scatter_rows(): lax.psum_scatter(value.astype(jnp.bfloat16), 'row', scatter_dimension=0,...  150 us
    reduce_scatter x2, waiting for transfers between devices, scatter_cols(): lax.psum_scatter(value.astype(jnp.bfloat16), 'col', scatter_dimension=0,...  81.7 us
    all_to_all x2, blocking collectives, recover_rails(): inter = lax.all_to_all(met_up, axis_name='row', split_axis=0, concat_axis=0)  41.9 us
    all_gather x1, waiting for transfers between devices, gather_cols(): return lax.all_gather(value, 'col', axis=0, tiled=True)  39.6 us
    all_gather x1, blocking collectives, gather_cols(): return lax.all_gather(value, 'col', axis=0, tiled=True)  26.2 us
    unnamed x13, local copies, waits for them, and re-layouts  11.9 us
  transfers between devices with their start and end apart: 5, of which 5 were waited for; matrix products, arithmetic and copies ran while one was open for 5% of the time, Pallas kernels for 0%

profile of v1, /device:TPU:2, one launch (start us, length us, event | category | flops | bytes accessed | tf_op | source)
XLA Modules:
  0.0 395.4 jit_solution(12888975152312111725)
XLA Ops:
  7.2 1.0 stack.13
  8.2 21.9 %all_to_all.10 = bf16[32,16,1024]{2,1,0:T(8,128)(2,1)S(1)} all-to-all(bf16[32,16,1024]{2,1,0:T(8,128)(2,1)S(1)} %stack.13), channel_id=1, replica_groups=mesh['row'=32,'col'=8] {'row'}, dimensions={0} | all-to-all | bytes 2097152 | tf_op jit(solution)/shard_map/all_to_all | solution.py:14
  30.1 5.3 %fusion.4 = bf16[512,2,896]{2,0,1:T(8,128)(2,1)} fusion(bf16[512,1024,1]{1,0,2:T(8,128)(2,1)S(1)} %bitcast.42, bf16[1024,2,896]{2,1,0:T(2,128)(2,1)} %param.5), kind=kOutput, calls=%fused_computation.6 | convolution fusion | flops 1879965696 | bytes 6553600 | tf_op jit(solution)/shard_map/td,dgf->tgf/dot_general | solution.py:50
  35.5 43.1 %reduce-scatter.5.cloned.1.call-done = bf16[64,2,896]{2,0,1:T(8,128)(2,1)} async-done(((bf16[512,2,896]{2,0,1:T(8,128)(2,1)}), bf16[64,2,896]{2,0,1:T(8,128)(2,1)}) %reduce-scatter.5.cloned.1.call-update) | async-done | bytes 229392 | tf_op jit(solution)/shard_map/reduce_scatter | solution.py:25
  78.6 1.0 convert_element_type.60
  79.6 26.2 %all_gather.6 = bf16[512,896]{1,0:T(8,128)(2,1)S(1)} all-gather(bf16[64,896]{1,0:T(8,128)(2,1)S(1)} %multiply_convert_fusion), channel_id=1, replica_groups=mesh['row'=32,'col'=8] {'col'}, dimensions={0}, use_global_device_ids=true | all-gather | bytes 1032192 | tf_op jit(solution)/shard_map/all_gather | solution.py:21
  105.8 0.9 copy-done.2
  106.8 2.3 convolution_convert_fusion.1
  109.1 84.2 %reduce-scatter.7.cloned.1.call-done = bf16[16,1024]{1,0:T(8,128)(2,1)} async-done(((bf16[512,1024]{1,0:T(8,128)(2,1)}), bf16[16,1024]{1,0:T(8,128)(2,1)}) %reduce-scatter.7.cloned.1.call-update) | async-done | bytes 32784 | tf_op jit(solution)/shard_map/reduce_scatter | solution.py:31
  193.3 1.4 subtract_convert_fusion
  194.7 0.1 stack.14
  194.8 20.1 %all_to_all.11 = bf16[32,16,1024]{2,1,0:T(8,128)(2,1)S(1)} all-to-all(bf16[32,16,1024]{2,1,0:T(8,128)(2,1)S(1)} %stack.14), channel_id=1, replica_groups=mesh['row'=32,'col'=8] {'row'}, dimensions={0} | all-to-all | bytes 2097152 | tf_op jit(solution)/shard_map/all_to_all | solution.py:14
  214.9 1.0 copy-done.1
  215.9 2.2 convolution_convert_fusion.2
  218.2 38.6 %reduce-scatter.9.cloned.1.call-done = bf16[64,896]{1,0:T(8,128)(2,1)} async-done(((bf16[512,896]{1,0:T(8,128)(2,1)}), bf16[64,896]{1,0:T(8,128)(2,1)}) %reduce-scatter.9.cloned.1.call-update) | async-done | bytes 114704 | tf_op jit(solution)/shard_map/reduce_scatter | solution.py:25
  256.8 1.0 fusion.15
  257.8 0.7 pad_maximum_fusion
  258.6 39.6 %all-gather.2.cloned.1.call-done = bf16[512,2,896]{2,0,1:T(8,128)(2,1)} async-done(((bf16[64,2,896]{2,0,1:T(8,128)(2,1)}), bf16[512,2,896]{2,0,1:T(8,128)(2,1)}) %all-gather.2.cloned.1.call-update) | async-done | bytes 1835024 | tf_op jit(solution)/shard_map/all_gather | solution.py:21
  298.2 5.7 %bitcast_convert_fusion = bf16[512,1024]{1,0:T(8,128)(2,1)} fusion(bf16[512,2,896]{2,0,1:T(8,128)(2,1)} %all-gather.2.cloned.1.call-done, bf16[1024,2,896]{2,1,0:T(2,128)(2,1)} %param.5), kind=kOutput, calls=%fused_computation.5 | convolution fusion | flops 1879572480 | bytes 6553600 | tf_op jit(solution)/shard_map/tgf,dgf->td/dot_general | solution.py:77
  303.9 4.0 %convolution_convert_fusion = bf16[896,1024]{1,0:T(8,128)(2,1)} fusion(bf16[512,896]{1,0:T(8,128)(2,1)} %copy-done.2, bf16[512,1024]{1,0:T(8,128)(2,1)} %bitcast.45), kind=kOutput, calls=%fused_computation.7 | convolution fusion | flops 940441600 | bytes 3801088 | tf_op jit(solution)/shard_map/tf,td->fd/dot_general | solution.py:67
  307.9 3.9 convert_bitcast_fusion
  311.9 10.0 %copy.10 = bf16[1024,2,896]{2,1,0:T(2,128)(2,1)} copy(bf16[1024,2,896]{0,2,1:T(8,128)(2,1)} %convert_bitcast_fusion) | data formatting | bytes 7340032
  321.8 65.7 %reduce-scatter.11.cloned.1.call-done = bf16[16,1024]{1,0:T(8,128)(2,1)} async-done(((bf16[512,1024]{1,0:T(8,128)(2,1)}), bf16[16,1024]{1,0:T(8,128)(2,1)}) %reduce-scatter.11.cloned.1.call-update) | async-done | bytes 32784 | tf_op jit(solution)/shard_map/reduce_scatter | solution.py:31
  387.5 1.4 add_convert_fusion
  (21 shorter events, 0.4 us)
Async XLA Ops:
  7.2 99.6 %copy-start = (bf16[896,1024]{1,0:T(8,128)(2,1)S(1)}, bf16[896,1024]{1,0:T(8,128)(2,1)}, u32[]{:S(2)}) copy-start(bf16[896,1024]{1,0:T(8,128)(2,1)} %param.6) | copy-start | bytes 5505028
  7.2 71.4 %reduce-scatter.5.cloned.1.call-start = ((), (), s32[]{:S(2)}) async-start(), calls=%async_computation.6 | async-start | bytes 2064384 | tf_op jit(solution)/shard_map/reduce_scatter | solution.py:25
  35.5 157.9 %reduce-scatter.7.cloned.1.call-start = ((), (), s32[]{:S(2)}) async-start(), calls=%async_computation.7 | async-start | bytes 1081344 | tf_op jit(solution)/shard_map/reduce_scatter | solution.py:31
  105.8 0.9 copy-start.2
  106.8 86.5 %copy-start.3 = (bf16[16,1024]{1,0:T(8,128)(2,1)S(1)}, bf16[16,1024]{1,0:T(8,128)(2,1)}, u32[]{:S(2)}) copy-start(bf16[16,1024]{1,0:T(8,128)(2,1)} %param.4) | copy-start | bytes 98308
  106.8 86.5 %copy-start.4 = (bf16[16,1024]{1,0:T(8,128)(2,1)S(1)}, bf16[16,1024]{1,0:T(8,128)(2,1)}, u32[]{:S(2)}) copy-start(bf16[16,1024]{1,0:T(8,128)(2,1)} %param.7) | copy-start | bytes 98308
  109.1 147.7 %reduce-scatter.9.cloned.1.call-start = ((), (), s32[]{:S(2)}) async-start(), calls=%async_computation.8 | async-start | bytes 1032192 | tf_op jit(solution)/shard_map/reduce_scatter | solution.py:25
  214.9 1.0 copy-start.1
  218.1 80.1 %all-gather.2.cloned.1.call-start = ((), (), s32[]{:S(2)}) async-start(), calls=%async_computation.9 | async-start | bytes 2064384 | tf_op jit(solution)/shard_map/all_gather | solution.py:21
  258.5 129.0 %reduce-scatter.11.cloned.1.call-start = ((), (), s32[]{:S(2)}) async-start(), calls=%async_computation.10 | async-start | bytes 1081344 | tf_op jit(solution)/shard_map/reduce_scatter | solution.py:31
  303.9 4.0 %copy-start.5 = (bf16[512,2,896]{2,0,1:T(8,128)(2,1)S(1)}, bf16[512,2,896]{2,0,1:T(8,128)(2,1)}, u32[]{:S(2)}) copy-start(bf16[512,2,896]{2,0,1:T(8,128)(2,1)} %all-gather.2.cloned.1.call-done) | copy-start | bytes 5505028
Sparse Core Ops, SparseCore 0:
  35.6 42.9 reduce-scatter.4
  109.2 84.0 reduce-scatter.6
  218.2 38.4 reduce-scatter.8
  259.0 39.1 all-gather.1
  304.0 83.3 reduce-scatter.10
